TPU v7x, 512 devices: a whole 4x4x16 slice. The times are simulated.
512 devices in a mesh: facet: 64 (over z, y), pol: 4 (over x), tm: 2 (over core).
Axes of the slice: x: 4, y: 4, z: 16, core: 2. Of those that a mesh axis runs over, the one named last changes fastest.
Arguments:
- tile_spectral_lines: bfloat16 [64, 4, 2, 64, 4096], P('facet', 'pol', None, 'tm'), may hold values from -6 to 6
- taper_leading_axis: bfloat16 [64, 2, 128, 512], P('facet', 'tm'), may hold values from -0.25 to 0.25
- taper_trailing_axis: bfloat16 [64, 2, 128, 512], P('facet', 'tm'), may hold values from -0.25 to 0.25
- depth_layer_factors: bfloat16 [64, 2, 2, 128], P('facet', 'tm'), may hold values from -4 to 4
- measured_correlations: float32 [64, 8, 2, 128], P('facet', None, 'tm', 'pol'), may hold values from -6 to 6
- visibility_groups_table: int32 [64, 2, 3, 8], P('facet', 'tm'), may hold values from 0 to 130815, as said below
- antenna_links: int32 [2, 130816], replicated, may hold values from 0 to 511, as said below
- complex_receiver_factors: float32 [256, 4, 512], replicated, may hold values from -5 to 5
Outputs:
- residual: float32 [64, 8, 2, 128], P('facet', None, 'tm', 'pol')
- gain_grad: float32 [512, 1024], P(('facet', 'pol', 'tm'))
Inputs may be any that keep to these rules, and one draw needn't show every extreme that they name: `visibility_groups_table`: for each subgrid and owner, every block has a channel below 256, a count of 1 or more, and baselines offset to offset + count - 1 below 130816; the counts of one owner sum to at most 128, and some owner reaches 128 in every draw. `antenna_links`: each baseline joins two different stations.
All inputs are finite; a program needn't handle non-finite values.
Results may differ from a plain program's by a relative error of at most 0.012.
Values may be sent and summed in bfloat16 or wider, within the bound.
No kernel may reach another device: no remote copies, remote signals or barrier semaphores. Data moves between devices by JAX's collectives and lax.ppermute only.
A program may use at most 192 MiB of HBM per device.

v0:
```python
import math
import jax
import jax.numpy as jnp
import numpy as np
from jax import lax
from jax.sharding import PartitionSpec as P

FGRID = 8
FS = 4096
MC = 64
SG = 512
NPOL = 4
NW = 2
NCH = 256
NST = 512
w_chirp = 0.37
grad_scale = 0.1
feed_first = np.array([0, 0, 1, 1])
feed_second = np.array([0, 1, 0, 1])


def laid_out(blocks, dim):
    blocks = jnp.moveaxis(blocks, 0, dim)
    lengths = blocks.shape
    return blocks.reshape(*lengths[:dim], lengths[dim] * lengths[dim + 1], *lengths[dim + 2 :])


def from_everyone(shard, axis):
    copies = jnp.broadcast_to(shard, (lax.axis_size(axis), *shard.shape))
    return lax.all_to_all(copies, axis, split_axis=0, concat_axis=0, tiled=True)


def collect(shard, axis, dim):
    return laid_out(from_everyone(shard, axis), dim)


def dft_table(length):
    indices = jnp.arange(length, dtype=jnp.int32)
    product = indices[:, None] * indices[None, :] % length
    angles = 2.0 * math.pi / length * product.astype(jnp.float32)
    factor = 1.0 / math.sqrt(length)
    return (
        (jnp.cos(angles) * factor).astype(jnp.bfloat16),
        (jnp.sin(angles) * factor).astype(jnp.bfloat16),
    )


def phase_table(left_size, right_size, length):
    left_index = jnp.arange(left_size, dtype=jnp.int32)
    right_index = jnp.arange(right_size, dtype=jnp.int32)
    product = left_index[:, None] * right_index[None, :] % length
    angles = 2.0 * math.pi / length * product.astype(jnp.float32)
    return (jnp.cos(angles), -jnp.sin(angles))


def chirp_phase(row_total, side_cells):
    across = (jnp.arange(row_total, dtype=jnp.int32) - side_cells // 2).astype(jnp.float32)
    downward = (jnp.arange(side_cells, dtype=jnp.int32) - side_cells // 2).astype(jnp.float32)
    return (
        w_chirp
        * (across[:, None] * across[:, None] + downward[None, :] * downward[None, :])
        / float(side_cells * side_cells)
    )


def make_planes(sub_real, sub_imag, phase_grid, layers):
    planes_list = []
    for plane_index in range(layers):
        angles = 2.0 * math.pi * plane_index * phase_grid
        cosine = jnp.cos(angles)
        sine_part = jnp.sin(angles)
        planes_list.append(
            jnp.stack(
                [sub_real * cosine - sub_imag * sine_part, sub_real * sine_part + sub_imag * cosine]
            ).astype(jnp.bfloat16)
        )
    return jnp.stack(planes_list)


def decode_slots(block_table, slot_index):
    channels = block_table[..., 0, :]
    offsets = block_table[..., 1, :]
    amounts = block_table[..., 2, :]
    starts = jnp.cumsum(amounts, axis=-1) - amounts
    relative = slot_index[:, None] - starts[..., None, :]
    member = ((relative >= 0) & (relative < amounts[..., None, :])).astype(jnp.int32)
    slot_live = jnp.sum(member, axis=-1)
    channel = jnp.sum(member * channels[..., None, :], axis=-1)
    antenna_couple = jnp.sum(member * (offsets[..., None, :] + relative), axis=-1)
    return (slot_live, channel, antenna_couple)


def model_terms(pred_re, pred_im, obs_re, obs_im, gain_first, gain_second, slot_live):
    first_re = gain_first[..., 2 * feed_first]
    first_im = gain_first[..., 2 * feed_first + 1]
    second_re = gain_second[..., 2 * feed_second]
    second_im = gain_second[..., 2 * feed_second + 1]
    both_re = first_re * second_re + first_im * second_im
    both_im = first_im * second_re - first_re * second_im
    model_re = both_re * pred_re - both_im * pred_im
    model_im = both_re * pred_im + both_im * pred_re
    alive_mask = slot_live.astype(jnp.float32)[..., None]
    resid_re = alive_mask * (obs_re - model_re)
    resid_im = alive_mask * (obs_im - model_im)
    cross_re = second_re * pred_re + second_im * pred_im
    cross_im = second_im * pred_re - second_re * pred_im
    lead_re = -(resid_re * cross_re - resid_im * cross_im)
    lead_im = -(resid_re * cross_im + resid_im * cross_re)
    along_re = first_re * pred_re - first_im * pred_im
    along_im = first_re * pred_im + first_im * pred_re
    trail_re = -(resid_re * along_re + resid_im * along_im)
    trail_im = -(resid_re * along_im - resid_im * along_re)
    leading = jnp.stack(
        [
            lead_re[..., 0] + lead_re[..., 1],
            lead_im[..., 0] + lead_im[..., 1],
            lead_re[..., 2] + lead_re[..., 3],
            lead_im[..., 2] + lead_im[..., 3],
        ],
        axis=-1,
    )
    trailing = jnp.stack(
        [
            trail_re[..., 0] + trail_re[..., 2],
            trail_im[..., 0] + trail_im[..., 2],
            trail_re[..., 1] + trail_re[..., 3],
            trail_im[..., 1] + trail_im[..., 3],
        ],
        axis=-1,
    )
    return (resid_re, resid_im, leading, trailing)


def degrid_block(layers, rows_u, rows_v, weights_w):
    spread_v = jnp.einsum("wcuv,nv->wcun", layers, rows_v, preferred_element_type=jnp.float32)
    along_u = jnp.sum(spread_v * jnp.transpose(rows_u).astype(jnp.float32)[None, None], axis=2)
    return jnp.sum(along_u * weights_w.astype(jnp.float32)[:, None, :], axis=0)


def on_device(
    tile_spectral_lines,
    taper_leading_axis,
    taper_trailing_axis,
    depth_layer_factors,
    measured_correlations,
    visibility_groups_table,
    antenna_links,
    complex_receiver_factors,
):
    careful = lax.Precision.HIGH
    facet_total = tile_spectral_lines.shape[0]
    row_share = tile_spectral_lines.shape[3]
    spread = FS // MC
    subgrids = lax.axis_size("facet")
    source = (
        tile_spectral_lines[:, 0].astype(jnp.float32).reshape(facet_total, 2, row_share, MC, spread)
    )
    source_re = source[:, 0]
    source_im = source[:, 1]
    inner_re, inner_im = phase_table(MC, MC, MC)
    section_re = jnp.einsum("fmar,ak->fmkr", source_re, inner_re, precision=careful) - jnp.einsum(
        "fmar,ak->fmkr", source_im, inner_im, precision=careful
    )
    section_im = jnp.einsum("fmar,ak->fmkr", source_re, inner_im, precision=careful) + jnp.einsum(
        "fmar,ak->fmkr", source_im, inner_re, precision=careful
    )
    twist_re, twist_im = phase_table(MC, spread, FS)
    turned_re = section_re * twist_re - section_im * twist_im
    turned_im = section_re * twist_im + section_im * twist_re
    outer_re, outer_im = phase_table(spread, subgrids, spread)
    factor = 1.0 / math.sqrt(FS)
    contrib_re = (
        jnp.einsum("fmkr,rs->sfmk", turned_re, outer_re, precision=careful)
        - jnp.einsum("fmkr,rs->sfmk", turned_im, outer_im, precision=careful)
    ) * factor
    contrib_im = (
        jnp.einsum("fmkr,rs->sfmk", turned_re, outer_im, precision=careful)
        + jnp.einsum("fmkr,rs->sfmk", turned_im, outer_re, precision=careful)
    ) * factor
    contrib = jnp.concatenate([contrib_re, contrib_im], axis=-1).astype(jnp.bfloat16)
    table_re, table_im = dft_table(SG)
    upper_half = jnp.concatenate([table_re, table_im], axis=1).reshape(FGRID, MC, 2 * SG)
    lower_half = jnp.concatenate([-table_im, table_re], axis=1).reshape(FGRID, MC, 2 * SG)
    stacked_table = jnp.stack([upper_half, lower_half], axis=1).reshape(FGRID, 2 * MC, 2 * SG)
    received = lax.all_to_all(contrib, "facet", split_axis=0, concat_axis=1, tiled=True)
    pieces = received.reshape(FGRID, FGRID, received.shape[2], 2 * MC)
    product = jnp.einsum("ijmc,jcv->imv", pieces, stacked_table, preferred_element_type=jnp.float32)
    half_rows = product.astype(jnp.bfloat16)
    whole_rows = collect(half_rows, "tm", 1).reshape(SG, 2 * SG)
    owners = lax.axis_size("tm")
    owner_index = lax.axis_index("tm")
    row_count = SG // owners
    slots_own = taper_leading_axis.shape[2]
    flat_u = taper_leading_axis.reshape(slots_own, SG)
    flat_v = taper_trailing_axis.reshape(slots_own, SG)
    flat_w = depth_layer_factors.reshape(NW, slots_own)
    first_row = owner_index * row_count
    part_re = lax.dynamic_slice_in_dim(table_re, first_row, row_count, 0)
    part_im = lax.dynamic_slice_in_dim(table_im, first_row, row_count, 0)
    upper_rows = jnp.dot(part_re, whole_rows, preferred_element_type=jnp.float32)
    lower_rows = jnp.dot(part_im, whole_rows, preferred_element_type=jnp.float32)
    sub_real = upper_rows[:, :SG] - lower_rows[:, SG:]
    sub_imag = upper_rows[:, SG:] + lower_rows[:, :SG]
    own_part = jnp.stack([sub_real, sub_imag]).astype(jnp.bfloat16)
    subgrid = collect(own_part, "tm", 1)
    layers = make_planes(subgrid[0], subgrid[1], chirp_phase(SG, SG), NW)
    predicted = degrid_block(layers, flat_u, flat_v, flat_w)
    regrouped = lax.all_to_all(predicted[None], "pol", split_axis=2, concat_axis=0, tiled=True)
    quarter = regrouped.shape[2]
    slot_index = lax.axis_index("pol") * quarter + jnp.arange(quarter, dtype=jnp.int32)
    slot_live, channel, antenna_couple = decode_slots(
        visibility_groups_table.reshape(3, visibility_groups_table.shape[3]), slot_index
    )
    antenna_left = jnp.take(antenna_links[0], antenna_couple)
    antenna_right = jnp.take(antenna_links[1], antenna_couple)
    gains_turned = jnp.transpose(complex_receiver_factors, (0, 2, 1))
    gain_first = gains_turned[channel, antenna_left]
    gain_second = gains_turned[channel, antenna_right]
    pred_re = jnp.transpose(regrouped[:, 0])
    pred_im = jnp.transpose(regrouped[:, 1])
    observed_local = measured_correlations.reshape(NPOL, 2, quarter)
    obs_re = jnp.transpose(observed_local[:, 0])
    obs_im = jnp.transpose(observed_local[:, 1])
    resid_re, resid_im, leading, trailing = model_terms(
        pred_re, pred_im, obs_re, obs_im, gain_first, gain_second, slot_live
    )
    residual = jnp.stack([jnp.transpose(resid_re), jnp.transpose(resid_im)], axis=1).reshape(
        1, 2 * NPOL, 1, quarter
    )
    channel_ids = jnp.arange(NCH, dtype=jnp.int32)
    own_count = NST // lax.axis_size(("facet", "pol", "tm"))
    own_stations = (
        lax.axis_index(("facet", "pol", "tm")) * own_count + jnp.arange(own_count, dtype=jnp.int32)
    ).astype(jnp.float32)
    channel_float = channel_ids.astype(jnp.float32)
    ident_rows = jnp.stack([antenna_left, antenna_right, channel]).astype(jnp.float32)
    records = jnp.concatenate([ident_rows, jnp.transpose(leading), jnp.transpose(trailing)], axis=0)
    piece = lax.all_gather(records, ("facet", "pol", "tm"), axis=1, tiled=True)
    piece_rows = piece.shape[1]
    group = math.gcd(piece_rows, 8 * quarter)
    grouped = jnp.transpose(piece.reshape(11, piece_rows // group, group), (1, 0, 2))

    def one_group(carry, record_block):
        match_first = (record_block[0][:, None] == own_stations[None, :]).astype(jnp.float32)
        match_second = (record_block[1][:, None] == own_stations[None, :]).astype(jnp.float32)
        weighted = (
            match_first[:, :, None] * jnp.transpose(record_block[3:7])[:, None, :]
            + match_second[:, :, None] * jnp.transpose(record_block[7:11])[:, None, :]
        )
        onehot = (record_block[2][:, None] == channel_float[None, :]).astype(jnp.float32)
        added = jnp.dot(
            jnp.transpose(weighted.reshape(group, own_count * 4)), onehot, precision=careful
        )
        return (carry + added.reshape(own_count, 4, NCH), None)

    result, unused = lax.scan(one_group, jnp.zeros((own_count, 4, NCH), jnp.float32), grouped)
    gain_grad = grad_scale * jnp.transpose(result, (0, 2, 1)).reshape(own_count, 4 * NCH)
    return (residual, gain_grad)


def solution(mesh):
    return jax.shard_map(
        on_device,
        mesh=mesh,
        in_specs=(
            P("facet", "pol", None, "tm", None),
            P("facet", "tm", None, None),
            P("facet", "tm", None, None),
            P("facet", "tm", None, None),
            P("facet", None, "tm", "pol"),
            P("facet", "tm", None, None),
            P(),
            P(),
        ),
        out_specs=(P("facet", None, "tm", "pol"), P(("facet", "pol", "tm"), None)),
        check_vma=False,
    )
```

profile of v0, /device:TPU:1, one launch (start us, length us, event | category | flops | bytes accessed | tf_op | source)
XLA Modules:
  0.0 288.2 jit_solution(2135503734819156724)
XLA Ops:
  0.6 2.1 reshape.857
  2.7 0.5 fusion.75
  3.3 0.5 fusion.76
  4.1 0.5 fusion.29
  4.7 0.5 fusion.30
  5.4 1.7 fusion.60
  7.1 1.7 fusion.58
  8.8 1.7 fusion.38
  10.5 1.7 fusion.37
  12.6 1.1 copy.72
  13.7 19.7 %all-to-all-start = ((bf16[64,1,32,128]{3,2,1,0:T(8,128)(2,1)}), bf16[64,1,32,128]{3,2,1,0:T(8,128)(2,1)}, u32[]{:S(2)}, u32[]{:S(2)}) async-start(bf16[64,1,32,128]{3,2,1,0:T(8,128)(2,1)} %copy.72), calls=%async_computation | async-start | bytes 1048576 | tf_op jit(solution)/shard_map/all_to_all | solution.py:185
  33.7 0.7 convert_reduce_fusion
  34.4 4.2 %slice_reduce_fusion.1 = (s32[130816]{0:T(1024)S(1)}, s32[130816]{0:T(1024)S(1)}) fusion(s32[2,130816]{1,0:T(2,128)} %param.26), kind=kLoop, calls=%fused_computation.123 | loop fusion | bytes 2093056 | tf_op jit(solution)/shard_map/slice | solution.py:214
  38.6 0.7 gather_fusion.6
  39.3 0.7 gather_fusion.7
  40.0 0.7 pad_clamp_fusion.3
  40.7 0.7 pad_clamp_fusion.1
  41.5 29.9 %copy.65 = f32[256,4,512]{1,2,0:T(8,128)} copy(f32[256,4,512]{2,1,0:T(4,128)S(1)} %copy-done.1) | data formatting | bytes 4194304 | tf_op args[7]
  71.4 1.4 gather_fusion
  72.9 0.6 gather_fusion.1
  73.4 0.6 gather_fusion.4
  74.0 2.0 gather_fusion.2
  76.0 0.6 add_convert_fusion
  76.6 0.6 pad_clamp_fusion.2
  77.2 0.6 pad_clamp_fusion
  78.3 4.3 %fusion.83 = bf16[8,1,64,512]{3,2,1,0:T(8,128)(2,1)S(1)} fusion(s32[8,64]{1,0:T(8,128)S(1)} %multiply_add_fusion.3), kind=kLoop, calls=%fused_computation.133 | loop fusion | flops 4980736 | bytes 526336 | tf_op jit(solution)/shard_map/neg | solution.py:183
  82.6 4.9 %multiply_convert_fusion = (bf16[8,1,64,512]{3,2,1,0:T(8,128)(2,1)S(1)}, bf16[8,1,64,512]{3,2,1,0:T(8,128)(2,1)S(1)}) fusion(s32[8,64]{1,0:T(8,128)S(1)} %multiply_add_fusion.3), kind=kLoop, calls=%fused_computation.96 | loop fusion | flops 4718592 | bytes 1050624 | tf_op jit(solution)/shard_map/convert_element_type | solution.py:44
  88.2 0.5 bitcast_convert_fusion
  88.7 0.6 fusion.197
  89.3 1.8 fusion.36
  91.2 5.1 %all_to_all.37 = bf16[2,8,32,1024]{3,2,1,0:T(8,128)(2,1)S(1)} all-to-all(bf16[2,8,32,1024]{3,2,1,0:T(8,128)(2,1)S(1)} %broadcast_in_dim.32), channel_id=1, replica_groups=mesh['facet'=64,'pol'=4,'tm'=2] {'tm'}, dimensions={0} | all-to-all | bytes 2097152 | tf_op jit(solution)/shard_map/all_to_all | solution.py:30
  96.4 2.0 fusion.77
  98.4 2.0 fusion.78
  100.9 4.7 %all_to_all.38 = bf16[2,2,256,512]{3,2,1,0:T(8,128)(2,1)S(1)} all-to-all(bf16[2,2,256,512]{3,2,1,0:T(8,128)(2,1)S(1)} %broadcast_in_dim.33), channel_id=1, replica_groups=mesh['facet'=64,'pol'=4,'tm'=2] {'tm'}, dimensions={0} | all-to-all | bytes 2097152 | tf_op jit(solution)/shard_map/all_to_all | solution.py:30
  105.6 8.5 %fusion.74 = (bf16[1,1,512,512]{3,2,1,0:T(8,128)(2,1)S(1)}, bf16[1,1,512,512]{3,2,1,0:T(8,128)(2,1)S(1)}, bf16[1,1,512,512]{3,2,1,0:T(8,128)(2,1)S(1)}, bf16[1,1,512,512]{3,2,1,0:T(8,128)(2,1)S(1)}) fusion(bf16[1,512,512]{2,1,0:T(8,128)(2,1)S(1)} %bitcast.376, f32[512]{0:T(512)S(1)} %convert_multiply_fusion.8, bf16[1,512,512]{2,1,0:T(8,128)(2,1)S(1)} %bitcast.375), kind=kLoop, calls=%fused_computation.121 | loop fusion | flops 5505024 | bytes 3147776 | tf_op jit(solution)/shard_map/stack | solution.py:73
  114.1 0.7 fusion.39
  114.9 0.7 copy.75
  115.6 5.1 %all-to-all-start.3 = ((f32[1,2,128]{1,0,2:T(1,128)}), f32[1,2,128]{1,0,2:T(1,128)S(1)}, u32[]{:S(2)}, u32[]{:S(2)}) async-start(f32[1,2,128]{1,0,2:T(1,128)} %copy.75), calls=%async_computation.3 | async-start | bytes 131072 | tf_op jit(solution)/shard_map/all_to_all | solution.py:208
  120.8 0.7 gather_fusion.3
  121.5 0.7 gather_fusion.5
  122.2 3.0 %all-to-all-done.3 = f32[1,2,128]{1,0,2:T(1,128)S(1)} async-done(((f32[1,2,128]{1,0,2:T(1,128)}), f32[1,2,128]{1,0,2:T(1,128)S(1)}, u32[]{:S(2)}, u32[]{:S(2)}) %all-to-all-start.3) | async-done | bytes 1056 | tf_op jit(solution)/shard_map/all_to_all | solution.py:208
  125.4 136.5 %all-gather = f32[512,32,11]{1,2,0:T(8,128)S(1)} all-gather(f32[1,32,11]{1,2,0:T(8,128)S(1)} %maximum_bitcast_fusion), channel_id=1, replica_groups=mesh['facet'=64,'pol'=4,'tm'=2] {'facet','pol','tm'}, dimensions={0}, use_global_device_ids=true | all-gather | bytes 722304 | tf_op jit(solution)/shard_map/all_gather | solution.py:238
  262.0 0.9 copy.79
  262.9 2.3 reshape.946
  265.2 1.5 copy.93
  266.8 19.9 %while.11 = (s32[]{:T(128)}, f32[1,4,256]{2,1,0:T(4,128)S(1)}, f32[64,11,256]{2,0,1:T(8,128)S(1)}, f32[1]{0:T(128)}, s32[]{:T(128)}, /*index=5*/s32[]{:T(128)}, s32[]{}, s32[]{}, s32[]{}, s32[]{}) while((s32[]{:T(128)}, f32[1,4,256]{2,1,0:T(4,128)S(1)}, f32[64,11,256]{2,0,1:T(8,128)S(1)}, f32[1]{0:T(128)}, s32[]{:T(128)}, ...), condition=%wide.region_7.9_spmd.clone, body=%wide.region_6.8_spmd.clone.sunk | while | flops 1644807 | bytes 44223 | solution.py:256
  286.9 0.7 mul.845
  287.6 0.6 copy.78
  (395 shorter events, 21.3 us)
Async XLA Ops:
  0.6 113.5 %copy-start = (bf16[1,1,128,512]{3,2,1,0:T(8,128)(2,1)S(1)}, bf16[1,1,128,512]{3,2,1,0:T(8,128)(2,1)}, u32[]{:S(2)}) copy-start(bf16[1,1,128,512]{3,2,1,0:T(8,128)(2,1)} %param.22) | copy-start | bytes 393220
  12.3 21.2 %copy-start.2 = (bf16[1,1,128,512]{3,2,1,0:T(8,128)(2,1)S(1)}, bf16[1,1,128,512]{3,2,1,0:T(8,128)(2,1)}, u32[]{:S(2)}) copy-start(bf16[1,1,128,512]{3,2,1,0:T(8,128)(2,1)} %param.21) | copy-start | bytes 393220
  12.3 21.2 %copy-start.8 = (s32[1,1,3,8]{3,1,2,0:T(1,128)S(1)}, s32[1,1,3,8]{3,1,2,0:T(1,128)}, u32[]{:S(2)}) copy-start(s32[1,1,3,8]{3,1,2,0:T(1,128)} %param.25) | copy-start | bytes 292
  13.7 75.6 %all-to-all-start = ((bf16[64,1,32,128]{3,2,1,0:T(8,128)(2,1)}), bf16[64,1,32,128]{3,2,1,0:T(8,128)(2,1)}, u32[]{:S(2)}, u32[]{:S(2)}) async-start(bf16[64,1,32,128]{3,2,1,0:T(8,128)(2,1)} %copy.72), calls=%async_computation | async-start | bytes 1048576 | tf_op jit(solution)/shard_map/all_to_all | solution.py:185
  33.5 8.0 %copy-start.1 = (f32[256,4,512]{2,1,0:T(4,128)S(1)}, f32[256,4,512]{2,1,0:T(4,128)}, u32[]{:S(2)}) copy-start(f32[256,4,512]{2,1,0:T(4,128)} %param.27) | copy-start | bytes 6291460
  41.5 35.1 %copy-start.11 = (s32[4]{0:T(128)S(1)}, s32[4]{0:T(128)}, u32[]{:S(2)}) copy-start(s32[4]{0:T(128)} %constant.187) | copy-start | bytes 52
  41.5 35.7 %copy-start.10 = (s32[4]{0:T(128)S(1)}, s32[4]{0:T(128)}, u32[]{:S(2)}) copy-start(s32[4]{0:T(128)} %constant.189) | copy-start | bytes 52
  87.5 0.7 copy-start.13
  87.5 1.2 copy-start.6
  114.1 0.8 copy-start.9
  114.1 6.6 %copy-start.3 = (f32[32,4]{1,0:T(8,128)S(1)}, f32[32,4]{1,0:T(8,128)}, u32[]{:S(2)}) copy-start(f32[32,4]{1,0:T(8,128)} %gather_fusion.2) | copy-start | bytes 1540
  114.1 8.1 %copy-start.12 = (s32[32]{0:T(128)S(1)}, s32[32]{0:T(128)}, u32[]{:S(2)}) copy-start(s32[32]{0:T(128)} %get-tuple-element.68) | copy-start | bytes 388
  114.1 11.2 %copy-start.4 = (f32[4,1,32]{2,1,0:T(1,128)S(1)}, f32[4,1,32]{2,1,0:T(1,128)}, u32[]{:S(2)}) copy-start(f32[4,1,32]{2,1,0:T(1,128)} %get-tuple-element.107) | copy-start | bytes 1540
  114.1 11.3 %copy-start.5 = (f32[3,32]{1,0:T(4,128)S(1)}, f32[3,32]{1,0:T(4,128)}, u32[]{:S(2)}) copy-start(f32[3,32]{1,0:T(4,128)} %add_convert_fusion) | copy-start | bytes 1156
  115.6 9.6 %all-to-all-start.3 = ((f32[1,2,128]{1,0,2:T(1,128)}), f32[1,2,128]{1,0,2:T(1,128)S(1)}, u32[]{:S(2)}, u32[]{:S(2)}) async-start(f32[1,2,128]{1,0,2:T(1,128)} %copy.75), calls=%async_computation.3 | async-start | bytes 131072 | tf_op jit(solution)/shard_map/all_to_all | solution.py:208
  265.2 1.6 copy-start.7
where the time goes:
time: 289 us; the launch traced here: 288 us
  blocking collectives  146 us (51%)
  local copies, waits for them, and re-layouts  55.5 us (19%)
  matrix products  30.4 us (11%)
  other arithmetic  24.8 us (9%)
  starting transfers between devices  24.8 us (9%)
  waiting for transfers between devices  3 us (1%)
    all_gather x1, blocking collectives, on_device(): piece = lax.all_gather(records, ('facet', 'pol', 'tm'), axis=1, tiled=True)  137 us
    unnamed x31, local copies, waits for them, and re-layouts  34.2 us
    all_to_all x1, starting transfers between devices, on_device(): lax.all_to_all(contrib, 'facet', split_axis=0, concat_axis=1, tiled=True)  19.7 us
    dot_general x64, matrix products, one_group(): jnp.dot(jnp.transpose(weighted.reshape(group, own_count * 4)), onehot, pr...  14.9 us
    all_to_all x2, blocking collectives, from_everyone(): return lax.all_to_all(copies, axis, split_axis=0, concat_axis=0, tiled=True)  9.81 us
    another operation x1, other arithmetic, make_planes(): jnp.stack([sub_real * cosine - sub_imag * sine_part, sub_real * sine_part...  8.45 us
  transfers between devices with their start and end apart: 2, of which 1 were waited for; matrix products, arithmetic and copies ran while one was open for 20% of the time, Pallas kernels for 0%

commit v1 on v0

--- a/solution.py
+++ b/solution.py
@@ -17,6 +17,17 @@
 grad_scale = 0.1
 feed_first = np.array([0, 0, 1, 1])
 feed_second = np.array([0, 1, 0, 1])
+
+
+def split_up(x, dim, size):
+    before, after = (x.shape[:dim], x.shape[dim + 1 :])
+    return jnp.moveaxis(x.reshape(*before, size, -1, *after), dim, 0)
+
+
+def in_order(blocks, dim):
+    dims = list(blocks.shape[1:])
+    dims[dim] *= blocks.shape[0]
+    return jnp.moveaxis(blocks, 0, dim).reshape(dims)
 
 
 def laid_out(blocks, dim):
@@ -205,7 +216,14 @@
     subgrid = collect(own_part, "tm", 1)
     layers = make_planes(subgrid[0], subgrid[1], chirp_phase(SG, SG), NW)
     predicted = degrid_block(layers, flat_u, flat_v, flat_w)
-    regrouped = lax.all_to_all(predicted[None], "pol", split_axis=2, concat_axis=0, tiled=True)
+    count, index = (lax.axis_size("pol"), lax.axis_index("pol"))
+    tiles = split_up(predicted[None], 2, count)
+    gathered = [tiles[index]]
+    for step in range(1, count):
+        sent = tiles[(index + step) % count]
+        gathered.append(lax.ppermute(sent, "pol", [(i, (i + step) % count) for i in range(count)]))
+    tiles = jnp.stack(gathered)[(index - jnp.arange(count)) % count]
+    regrouped = in_order(tiles, 0)
     quarter = regrouped.shape[2]
     slot_index = lax.axis_index("pol") * quarter + jnp.arange(quarter, dtype=jnp.int32)
     slot_live, channel, antenna_couple = decode_slots(

time: 289 us -> 296 us (1.024)
  starting transfers between devices: 24.8 us -> 31.2 us
    ppermute x0 -> x3, starting transfers between devices: none -> 11.5 us  [on_device(): lax.ppermute(sent, 'pol', [(i, (i + step) % count) for i in range(count)])]
    all_to_all x1 -> x0, starting transfers between devices: 5.1 us -> none  [on_device(): lax.all_to_all(predicted[None], 'pol', split_axis=2, concat_axis=0, tiled...]
    all_to_all x1 -> x0, waiting for transfers between devices: 3 us -> none  [on_device(): lax.all_to_all(predicted[None], 'pol', split_axis=2, concat_axis=0, tiled...]
    unnamed x31 -> x33, local copies, waits for them, and re-layouts: 34.2 us -> 34.1 us
  transfers between devices with their start and end apart: 2 -> 4, of which waited for: 1 -> 1; matrix products, arithmetic and copies ran while one was open for 20% -> 20% of each run, Pallas kernels for 0% -> 0%
where the time goes in v1:
time: 296 us
  blocking collectives  148 us (50%)
  local copies, waits for them, and re-layouts  54.6 us (18%)
  starting transfers between devices  31.2 us (11%)
  matrix products  30.4 us (10%)
  other arithmetic  27.3 us (9%)
    all_gather x1, blocking collectives, on_device(): piece = lax.all_gather(records, ('facet', 'pol', 'tm'), axis=1, tiled=True)  138 us
    unnamed x33, local copies, waits for them, and re-layouts  34.1 us
    all_to_all x1, starting transfers between devices, on_device(): lax.all_to_all(contrib, 'facet', split_axis=0, concat_axis=1, tiled=True)  19.7 us
    dot_general x64, matrix products, one_group(): jnp.dot(jnp.transpose(weighted.reshape(group, own_count * 4)), onehot, pr...  14.9 us
    ppermute x3, starting transfers between devices, on_device(): lax.ppermute(sent, 'pol', [(i, (i + step) % count) for i in range(count)])  11.5 us
    all_to_all x2, blocking collectives, from_everyone(): return lax.all_to_all(copies, axis, split_axis=0, concat_axis=0, tiled=True)  9.89 us
    another operation x1, other arithmetic, make_planes(): jnp.stack([sub_real * cosine - sub_imag * sine_part, sub_real * sine_part...  8.45 us
  transfers between devices with their start and end apart: 4, of which 1 were waited for; matrix products, arithmetic and copies ran while one was open for 20% of the time, Pallas kernels for 0%

profile of v1, /device:TPU:1, one launch (start us, length us, event | category | flops | bytes accessed | tf_op | source)
XLA Modules:
  0.0 295.7 jit_solution(11809676976456121613)
XLA Ops:
  0.6 2.1 reshape.916
  5.4 1.7 fusion.60
  7.1 1.7 fusion.58
  8.8 1.7 fusion.38
  10.5 1.7 fusion.37
  12.6 1.2 copy.71
  13.7 19.7 %all-to-all-start = ((bf16[64,1,32,128]{3,2,1,0:T(8,128)(2,1)}), bf16[64,1,32,128]{3,2,1,0:T(8,128)(2,1)}, u32[]{:S(2)}, u32[]{:S(2)}) async-start(bf16[64,1,32,128]{3,2,1,0:T(8,128)(2,1)} %copy.71), calls=%async_computation | async-start | bytes 1048576 | tf_op jit(solution)/shard_map/all_to_all | solution.py:196
  33.7 0.6 convert_reduce_fusion
  34.4 4.2 %slice_reduce_fusion.1 = (s32[130816]{0:T(1024)S(1)}, s32[130816]{0:T(1024)S(1)}) fusion(s32[2,130816]{1,0:T(2,128)} %param.26), kind=kLoop, calls=%fused_computation.124 | loop fusion | bytes 2093056 | tf_op jit(solution)/shard_map/slice | solution.py:232
  38.6 0.7 gather_fusion.7
  39.3 0.7 gather_fusion.8
  40.0 0.7 pad_clamp_fusion.4
  40.6 0.7 pad_clamp_fusion.2
  41.3 0.7 pad_clamp_fusion.3
  42.0 0.7 pad_clamp_fusion.1
  42.8 29.9 %copy.64 = f32[256,4,512]{1,2,0:T(8,128)} copy(f32[256,4,512]{2,1,0:T(4,128)S(1)} %copy-done.1) | data formatting | bytes 4194304 | tf_op args[7]
  72.7 1.3 gather_fusion
  74.1 0.6 gather_fusion.1
  74.6 0.6 gather_fusion.4
  75.2 1.3 gather_fusion.2
  76.6 0.6 gather_fusion.3
  77.2 0.6 gather_fusion.5
  77.7 0.5 convert_element_type.323
  78.3 0.6 convert_multiply_fusion.8
  78.9 1.3 add_convert_fusion
  80.2 0.6 pad_clamp_fusion
  81.3 4.3 %fusion.83 = bf16[8,1,64,512]{3,2,1,0:T(8,128)(2,1)S(1)} fusion(s32[8,64]{1,0:T(8,128)S(1)} %multiply_add_fusion.3), kind=kLoop, calls=%fused_computation.134 | loop fusion | flops 4980736 | bytes 526336 | tf_op jit(solution)/shard_map/neg | solution.py:194
  85.6 4.9 %multiply_convert_fusion = (bf16[8,1,64,512]{3,2,1,0:T(8,128)(2,1)S(1)}, bf16[8,1,64,512]{3,2,1,0:T(8,128)(2,1)S(1)}) fusion(s32[8,64]{1,0:T(8,128)S(1)} %multiply_add_fusion.3), kind=kLoop, calls=%fused_computation.97 | loop fusion | flops 4718592 | bytes 1050624 | tf_op jit(solution)/shard_map/convert_element_type | solution.py:55
  91.7 0.6 fusion.191
  92.3 1.7 fusion.36
  94.2 5.2 %all_to_all.19 = bf16[2,8,32,1024]{3,2,1,0:T(8,128)(2,1)S(1)} all-to-all(bf16[2,8,32,1024]{3,2,1,0:T(8,128)(2,1)S(1)} %broadcast_in_dim.30), channel_id=1, replica_groups=mesh['facet'=64,'pol'=4,'tm'=2] {'tm'}, dimensions={0} | all-to-all | bytes 2097152 | tf_op jit(solution)/shard_map/all_to_all | solution.py:41
  99.5 2.0 fusion.77
  101.5 2.0 fusion.78
  104.0 4.7 %all_to_all.20 = bf16[2,2,256,512]{3,2,1,0:T(8,128)(2,1)S(1)} all-to-all(bf16[2,2,256,512]{3,2,1,0:T(8,128)(2,1)S(1)} %broadcast_in_dim.31), channel_id=1, replica_groups=mesh['facet'=64,'pol'=4,'tm'=2] {'tm'}, dimensions={0} | all-to-all | bytes 2097152 | tf_op jit(solution)/shard_map/all_to_all | solution.py:41
  108.7 8.4 %fusion.74 = (bf16[1,1,512,512]{3,2,1,0:T(8,128)(2,1)S(1)}, bf16[1,1,512,512]{3,2,1,0:T(8,128)(2,1)S(1)}, bf16[1,1,512,512]{3,2,1,0:T(8,128)(2,1)S(1)}, bf16[1,1,512,512]{3,2,1,0:T(8,128)(2,1)S(1)}) fusion(bf16[1,512,512]{2,1,0:T(8,128)(2,1)S(1)} %bitcast.338, f32[512]{0:T(512)S(1)} %copy-done.3, bf16[1,512,512]{2,1,0:T(8,128)(2,1)S(1)} %bitcast.337), kind=kLoop, calls=%fused_computation.122 | loop fusion | flops 5505024 | bytes 3147776 | tf_op jit(solution)/shard_map/stack | solution.py:84
  117.2 0.7 fusion.39
  118.1 3.1 %collective-permute-start = (f32[1,2,32]{2,1,0:T(2,128)S(1)}, f32[1,2,32]{2,1,0:T(2,128)S(1)}, u32[]{:S(2)}, u32[]{:S(2)}) collective-permute-start(f32[1,2,32]{2,1,0:T(2,128)S(1)} %bitcast.358), channel_id=1, source_target_pairs={{0,2},{2,4},{4,6},{6,0},{1,3},{3,5},{5,7},{7,1},{8,10},{10,12},{12... | collective-permute-start | bytes 776 | tf_op jit(solution)/shard_map/ppermute | solution.py:224
  121.2 5.3 %collective-permute-start.1 = (f32[1,2,32]{2,1,0:T(2,128)S(1)}, f32[1,2,32]{2,1,0:T(2,128)S(1)}, u32[]{:S(2)}, u32[]{:S(2)}) collective-permute-start(f32[1,2,32]{2,1,0:T(2,128)S(1)} %bitcast.357), channel_id=1, source_target_pairs={{0,4},{2,6},{4,0},{6,2},{1,5},{3,7},{5,1},{7,3},{8,12},{10,14},{12... | collective-permute-start | bytes 776 | tf_op jit(solution)/shard_map/ppermute | solution.py:224
  126.5 3.1 %collective-permute-start.2 = (f32[1,2,32]{2,1,0:T(2,128)S(1)}, f32[1,2,32]{2,1,0:T(2,128)S(1)}, u32[]{:S(2)}, u32[]{:S(2)}) collective-permute-start(f32[1,2,32]{2,1,0:T(2,128)S(1)} %bitcast.356), channel_id=1, source_target_pairs={{0,6},{2,0},{4,2},{6,4},{1,7},{3,1},{5,3},{7,5},{8,14},{10,8},{12,... | collective-permute-start | bytes 776 | tf_op jit(solution)/shard_map/ppermute | solution.py:224
  129.6 1.2 collective-permute-done.2
  130.8 0.7 gather_fusion.6
  131.7 137.7 %all-gather = f32[512,32,11]{1,2,0:T(8,128)S(1)} all-gather(f32[1,32,11]{1,2,0:T(8,128)S(1)} %maximum_bitcast_fusion), channel_id=1, replica_groups=mesh['facet'=64,'pol'=4,'tm'=2] {'facet','pol','tm'}, dimensions={0}, use_global_device_ids=true | all-gather | bytes 722304 | tf_op jit(solution)/shard_map/all_gather | solution.py:256
  269.4 0.9 copy.76
  270.3 2.3 reshape.1017
  272.6 1.6 copy.90
  274.2 19.9 %while.11 = (s32[]{:T(128)}, f32[1,4,256]{2,1,0:T(4,128)S(1)}, f32[64,11,256]{2,0,1:T(8,128)S(1)}, f32[1]{0:T(128)}, s32[]{:T(128)}, /*index=5*/s32[]{:T(128)}, s32[]{}, s32[]{}, s32[]{}, s32[]{}) while((s32[]{:T(128)}, f32[1,4,256]{2,1,0:T(4,128)S(1)}, f32[64,11,256]{2,0,1:T(8,128)S(1)}, f32[1]{0:T(128)}, s32[]{:T(128)}, ...), condition=%wide.region_7.9_spmd.clone, body=%wide.region_6.8_spmd.clone.sunk | while | flops 1644807 | bytes 44223 | solution.py:274
  294.3 0.7 mul.845
  295.1 0.6 copy.75
  (406 shorter events, 24.0 us)
Async XLA Ops:
  0.6 116.6 %copy-start = (bf16[1,1,128,512]{3,2,1,0:T(8,128)(2,1)S(1)}, bf16[1,1,128,512]{3,2,1,0:T(8,128)(2,1)}, u32[]{:S(2)}) copy-start(bf16[1,1,128,512]{3,2,1,0:T(8,128)(2,1)} %param.22) | copy-start | bytes 393220
  12.3 21.2 %copy-start.2 = (bf16[1,1,128,512]{3,2,1,0:T(8,128)(2,1)S(1)}, bf16[1,1,128,512]{3,2,1,0:T(8,128)(2,1)}, u32[]{:S(2)}) copy-start(bf16[1,1,128,512]{3,2,1,0:T(8,128)(2,1)} %param.21) | copy-start | bytes 393220
  12.3 21.3 %copy-start.11 = (s32[1,1,3,8]{3,1,2,0:T(1,128)S(1)}, s32[1,1,3,8]{3,1,2,0:T(1,128)}, u32[]{:S(2)}) copy-start(s32[1,1,3,8]{3,1,2,0:T(1,128)} %param.25) | copy-start | bytes 292
  13.7 78.6 %all-to-all-start = ((bf16[64,1,32,128]{3,2,1,0:T(8,128)(2,1)}), bf16[64,1,32,128]{3,2,1,0:T(8,128)(2,1)}, u32[]{:S(2)}, u32[]{:S(2)}) async-start(bf16[64,1,32,128]{3,2,1,0:T(8,128)(2,1)} %copy.71), calls=%async_computation | async-start | bytes 1048576 | tf_op jit(solution)/shard_map/all_to_all | solution.py:196
  33.5 9.3 %copy-start.1 = (f32[256,4,512]{2,1,0:T(4,128)S(1)}, f32[256,4,512]{2,1,0:T(4,128)}, u32[]{:S(2)}) copy-start(f32[256,4,512]{2,1,0:T(4,128)} %param.27) | copy-start | bytes 6291460
  34.3 38.3 %copy-start.7 = (s32[32]{0:T(128)}, s32[32]{0:T(128)S(1)}, u32[]{:S(2)}) copy-start(s32[32]{0:T(128)S(1)} %get-tuple-element.69) | copy-start | bytes 388
  42.8 35.0 %copy-start.13 = (s32[32]{0:T(128)S(1)}, s32[32]{0:T(128)}, u32[]{:S(2)}) copy-start(s32[32]{0:T(128)} %get-tuple-element.68) | copy-start | bytes 388
  90.5 0.7 copy-start.14
  90.5 1.2 copy-start.8
  104.0 4.8 %copy-start.3 = (f32[512]{0:T(512)S(1)}, f32[512]{0:T(512)}, u32[]{:S(2)}) copy-start(f32[512]{0:T(512)} %convert_multiply_fusion.8) | copy-start | bytes 6148
  117.2 0.8 copy-start.12
  117.2 14.3 %copy-start.4 = (f32[4,1,32]{2,1,0:T(1,128)S(1)}, f32[4,1,32]{2,1,0:T(1,128)}, u32[]{:S(2)}) copy-start(f32[4,1,32]{2,1,0:T(1,128)} %get-tuple-element.106) | copy-start | bytes 1540
  117.2 14.3 %copy-start.5 = (f32[4,1,32]{2,1,0:T(1,128)S(1)}, f32[4,1,32]{2,1,0:T(1,128)}, u32[]{:S(2)}) copy-start(f32[4,1,32]{2,1,0:T(1,128)} %get-tuple-element.107) | copy-start | bytes 1540
  117.2 14.3 %copy-start.10 = (f32[32]{0:T(128)S(1)}, f32[32]{0:T(128)}, u32[]{:S(2)}) copy-start(f32[32]{0:T(128)} %convert_element_type.323) | copy-start | bytes 388
  117.2 14.5 %copy-start.6 = (f32[3,32]{1,0:T(4,128)S(1)}, f32[3,32]{1,0:T(4,128)}, u32[]{:S(2)}) copy-start(f32[3,32]{1,0:T(4,128)} %add_convert_fusion) | copy-start | bytes 1156
  118.1 11.5 %collective-permute-start = (f32[1,2,32]{2,1,0:T(2,128)S(1)}, f32[1,2,32]{2,1,0:T(2,128)S(1)}, u32[]{:S(2)}, u32[]{:S(2)}) collective-permute-start(f32[1,2,32]{2,1,0:T(2,128)S(1)} %bitcast.358), channel_id=1, source_target_pairs={{0,2},{2,4},{4,6},{6,0},{1,3},{3,5},{5,7},{7,1},{8,10},{10,12},{12... | collective-permute-start | bytes 776 | tf_op jit(solution)/shard_map/ppermute | solution.py:224
  121.2 8.4 %collective-permute-start.1 = (f32[1,2,32]{2,1,0:T(2,128)S(1)}, f32[1,2,32]{2,1,0:T(2,128)S(1)}, u32[]{:S(2)}, u32[]{:S(2)}) collective-permute-start(f32[1,2,32]{2,1,0:T(2,128)S(1)} %bitcast.357), channel_id=1, source_target_pairs={{0,4},{2,6},{4,0},{6,2},{1,5},{3,7},{5,1},{7,3},{8,12},{10,14},{12... | collective-permute-start | bytes 776 | tf_op jit(solution)/shard_map/ppermute | solution.py:224
  126.5 4.3 %collective-permute-start.2 = (f32[1,2,32]{2,1,0:T(2,128)S(1)}, f32[1,2,32]{2,1,0:T(2,128)S(1)}, u32[]{:S(2)}, u32[]{:S(2)}) collective-permute-start(f32[1,2,32]{2,1,0:T(2,128)S(1)} %bitcast.356), channel_id=1, source_target_pairs={{0,6},{2,0},{4,2},{6,4},{1,7},{3,1},{5,3},{7,5},{8,14},{10,8},{12,... | collective-permute-start | bytes 776 | tf_op jit(solution)/shard_map/ppermute | solution.py:224
  272.6 1.6 copy-start.9
